TPU v7x, 256 devices: a whole 4x4x8 slice. The times are simulated.
256 devices in a mesh: loop: 4 (over y_hi, core), inner: 64 (over z, x, y_lo).
Axes of the slice: x: 4, y: 4 (y_hi: 2, y_lo: 2; y = y_hi * 2 + y_lo), z: 8, core: 2. Of those that a mesh axis runs over, the one named last changes fastest.
Arguments:
- snapshots: bfloat16 [65536, 1024], P(('loop', 'inner')), may hold values from -6 to 6
- bins: int32 [65536], replicated, may hold values from 0 to 511, as said below
- pairs: int32 [2048, 2], replicated, may hold values from 0 to 511, as said below
- start_weights: bfloat16 [1024, 32], replicated, may hold values from -0.1875 to 0.1875
Outputs:
- basis: float32 [65536, 96], P(('loop', 'inner'))
- coefficients: float32 [4, 32, 32], replicated
Inputs may be any that keep to these rules, and one draw needn't show every extreme that they name: `bins`: the snapshot in row n has a bin in [r * 8, (r + 1) * 8), where r = (n // 256) mod (64). `pairs`: every row (a, b) has a <= b <= a + 8; every bin is paired with itself.
All inputs are finite; a program needn't handle non-finite values.
Results may differ from a plain program's by a relative error of at most 0.0003.
Values may be sent and summed in bfloat16 or wider, within the bound.
A program may use at most 64 MiB of HBM per device.

v0:
```python
import jax
import jax.numpy as jnp
from jax import lax
from jax.sharding import PartitionSpec as P

STEPS = 2
BINS_COL = 8


def extended(cells, sides, width):
    for axis, dim in sides:
        count = lax.axis_size(axis)
        ends = count - 1
        head = lax.slice_in_dim(cells, 0, width, axis=dim)
        tail = lax.slice_in_dim(cells, cells.shape[dim] - width, cells.shape[dim], axis=dim)
        cells = jnp.concatenate(
            [
                lax.ppermute(tail, axis, [(i, (i + 1) % count) for i in range(ends)]),
                cells,
                lax.ppermute(head, axis, [((i + 1) % count, i) for i in range(ends)]),
            ],
            axis=dim,
        )
    return cells


def matches(values, targets):
    return (values[:, None] == targets[None, :]).astype(jnp.float32)


def local_gram(left, right):
    return jnp.dot(left.T, right, precision=lax.Precision.HIGHEST)


def finish(matrix, gram_total):
    lower_factor = jnp.linalg.cholesky(gram_total)
    result = lax.linalg.triangular_solve(
        lower_factor, matrix, left_side=False, lower=True, transpose_a=True
    )
    return (result, lower_factor.T)


def local(snapshots, bins, pairs, start_weights):
    row_count, features = snapshots.shape
    block_width = start_weights.shape[1]
    n_loop = lax.axis_size("loop")
    n_inner = lax.axis_size("inner")
    column = lax.axis_index("inner")
    group = lax.axis_index("loop")
    bin_grid = jnp.pad(
        bins.reshape(n_loop, n_inner, row_count), ((0, 0), (1, 1), (0, 0)), constant_values=-1
    )
    stacked = lax.all_gather(snapshots[None], "loop", axis=0, tiled=True)
    partner_rows = extended(stacked, (("inner", 1),), row_count)
    tile_rows = partner_rows.reshape(n_loop * 3 * row_count, features)
    tile_bins = lax.dynamic_slice_in_dim(bin_grid, column, 3, 1).reshape(-1)
    my_bins = lax.dynamic_slice_in_dim(bins, (group * n_inner + column) * row_count, row_count)
    bin_base = column * BINS_COL
    my_ids = bin_base + jnp.arange(BINS_COL, dtype=jnp.int32)
    window_ids = bin_base - BINS_COL + jnp.arange(3 * BINS_COL, dtype=jnp.int32)
    left_bins = pairs[:, 0]
    right_bins = pairs[:, 1]
    pair_count = jnp.dot(
        matches(left_bins, my_ids).T,
        matches(right_bins, window_ids),
        precision=lax.Precision.HIGHEST,
    )
    pair_count = pair_count + jnp.dot(
        matches(right_bins, my_ids).T,
        matches(left_bins, window_ids),
        precision=lax.Precision.HIGHEST,
    )
    linked_bins = jnp.where(pair_count > 0.5, 1.0, 0.0).astype(jnp.float32)
    my_hot = matches(my_bins, my_ids)
    row_links = jnp.dot(my_hot, linked_bins)
    mine_wide = snapshots.astype(jnp.float32)
    mine_norms = jnp.sum(mine_wide * mine_wide, axis=1)
    epsilon = features / 3.0
    part_hot = matches(tile_bins, window_ids) * (tile_bins >= 0).astype(jnp.float32)[:, None]
    band_mask = jnp.dot(row_links, part_hot.T)
    part_wide = tile_rows.astype(jnp.float32)
    part_norms = jnp.sum(part_wide * part_wide, axis=1)
    products = lax.dot_general(
        snapshots, tile_rows, (((1,), (1,)), ((), ())), preferred_element_type=jnp.float32
    )
    distance = mine_norms[:, None] + part_norms[None, :] - 2.0 * products
    kept_tiles = [band_mask * jnp.exp(-distance / epsilon)]

    def current_kernel(which):
        return kept_tiles[which]

    degree = jnp.sum(current_kernel(0), axis=1)
    inv_root = lax.rsqrt(degree)
    start_block = jnp.dot(snapshots, start_weights, preferred_element_type=jnp.float32)
    start_total = lax.psum(local_gram(start_block, start_block), ("loop", "inner"))
    current, unused = finish(start_block, start_total)
    basis_blocks = [current]
    coefficients = []
    previous = current
    prev_b = jnp.zeros((block_width, block_width), jnp.float32)
    for lanczos_step in range(STEPS):
        scaled = inv_root[:, None] * current
        vec_stack = lax.all_gather(scaled[None], "loop", axis=0, tiled=True)
        vec_strip = extended(vec_stack, (("inner", 1),), row_count)
        strip = vec_strip.reshape(n_loop * 3 * row_count, block_width)
        total = jnp.dot(current_kernel(0), strip, precision=lax.Precision.HIGHEST)
        image = inv_root[:, None] * total
        projected = lax.psum(local_gram(current, image), ("loop", "inner"))
        image = image - jnp.dot(current, projected, precision=lax.Precision.HIGHEST)
        if lanczos_step > 0:
            image = image - jnp.dot(previous, prev_b.T, precision=lax.Precision.HIGHEST)
        gram_total = lax.psum(local_gram(image, image), ("loop", "inner"))
        following, factor = finish(image, gram_total)
        coefficients.append(projected)
        coefficients.append(factor)
        previous = current
        prev_b = factor
        current = following
        basis_blocks.append(current)
    return (jnp.concatenate(basis_blocks, axis=1), jnp.stack(coefficients))


def solution(mesh):
    in_specs = (P(("loop", "inner"), None), P(), P(), P())
    out_specs = (P(("loop", "inner"), None), P())
    return jax.shard_map(local, mesh=mesh, in_specs=in_specs, out_specs=out_specs, check_vma=False)
```

profile of v0, /device:TPU:1, one launch (start us, length us, event | category | flops | bytes accessed | tf_op | source)
XLA Modules:
  0.0 579.3 jit_solution(10393950573843033094)
XLA Ops:
  7.2 0.7 all-gather.5.cloned.1.call-update
  7.9 1.0 reshape.51
  9.0 0.8 dynamic_slice.6
  9.8 1.3 fusion.49
  11.2 90.2 %psum.35 = f32[32,32]{0,1:T(8,128)S(1)} all-reduce(f32[32,32]{0,1:T(8,128)S(1)} %fusion.50), channel_id=1, replica_groups=mesh['loop'=4,'inner'=64] {'loop','inner'}, use_global_device_ids=true, to_apply=%region_0.1 | all-reduce | flops 1024 | bytes 8192 | tf_op jit(solution)/shard_map/psum | solution.py:95
  101.5 1.3 collective-permute-start.1
  102.8 5.3 collective-permute-start
  108.1 2.9 cholesky.59
  111.1 0.6 compare_reduce_fusion.2
  111.7 0.7 fusion.30
  112.4 2.4 custom-call.7
  114.8 1.2 multiply_reduce_fusion.1
  116.1 0.8 fusion.45
  116.9 1.0 fusion.7
  117.9 1.0 fusion.4
  118.8 31.0 %collective-permute-done.1 = bf16[4,256,1024]{2,1,0:T(8,128)(2,1)S(1)} collective-permute-done((bf16[4,256,1024]{2,1,0:T(8,128)(2,1)}, bf16[4,256,1024]{2,1,0:T(8,128)(2,1)S(1)}, u32[]{:S(2)}, u32[]{:S(2)}) %collective-permute-start.1) | collective-permute-done | bytes 2097184 | tf_op jit(solution)/shard_map/ppermute | solution.py:20
  149.8 44.7 %collective-permute-done = bf16[4,256,1024]{2,1,0:T(8,128)(2,1)} collective-permute-done((bf16[4,256,1024]{2,1,0:T(8,128)(2,1)}, bf16[4,256,1024]{2,1,0:T(8,128)(2,1)}, u32[]{:S(2)}, u32[]{:S(2)}) %collective-permute-start) | collective-permute-done | bytes 2097184 | tf_op jit(solution)/shard_map/ppermute | solution.py:18
  194.5 3.6 multiply_reduce_fusion
  198.2 3.5 fusion
  201.7 3.1 fusion.46
  205.0 7.2 %all-gather.1 = f32[1024,32]{0,1:T(8,128)S(1)} all-gather(f32[256,32]{0,1:T(8,128)S(1)} %get-tuple-element.20), channel_id=3, replica_groups=mesh['loop'=4,'inner'=64] {'loop'}, dimensions={0}, use_global_device_ids=true | all-gather | bytes 163840 | tf_op jit(solution)/shard_map/all_gather | solution.py:103
  212.3 1.3 collective-permute-start.3
  213.6 4.8 collective-permute-start.2
  218.4 1.9 collective-permute-done.3
  220.2 3.2 collective-permute-done.2
  223.6 2.8 convolution_multiply_fusion.3
  226.5 80.3 %psum.36 = f32[32,32]{0,1:T(8,128)S(1)} all-reduce(f32[32,32]{0,1:T(8,128)S(1)} %fusion.51), channel_id=1, replica_groups=mesh['loop'=4,'inner'=64] {'loop','inner'}, use_global_device_ids=true, to_apply=%region_6.9 | all-reduce | flops 1024 | bytes 8192 | tf_op jit(solution)/shard_map/psum | solution.py:108
  307.2 75.5 %psum.37 = f32[32,32]{0,1:T(8,128)S(1)} all-reduce(f32[32,32]{0,1:T(8,128)S(1)} %fusion.52), channel_id=1, replica_groups=mesh['loop'=4,'inner'=64] {'loop','inner'}, use_global_device_ids=true, to_apply=%region_7.10 | all-reduce | flops 1024 | bytes 8192 | tf_op jit(solution)/shard_map/psum | solution.py:112
  382.8 2.9 cholesky.70
  385.8 0.6 compare_reduce_fusion.1
  386.4 1.2 fusion.38
  387.6 2.4 custom-call.8
  390.0 0.2 broadcast_multiply_fusion
  390.3 7.4 %all-gather.2 = f32[1024,32]{0,1:T(8,128)S(1)} all-gather(f32[256,32]{0,1:T(8,128)S(1)} %get-tuple-element.22), channel_id=4, replica_groups=mesh['loop'=4,'inner'=64] {'loop'}, dimensions={0}, use_global_device_ids=true | all-gather | bytes 163840 | tf_op jit(solution)/shard_map/all_gather | solution.py:103
  397.8 1.3 collective-permute-start.5
  399.1 4.0 collective-permute-start.4
  403.1 1.5 collective-permute-done.5
  404.7 2.6 collective-permute-done.4
  407.5 3.5 convolution_multiply_fusion.2
  411.1 76.5 %psum.38 = f32[32,32]{0,1:T(8,128)S(1)} all-reduce(f32[32,32]{0,1:T(8,128)S(1)} %fusion.53), channel_id=1, replica_groups=mesh['loop'=4,'inner'=64] {'loop','inner'}, use_global_device_ids=true, to_apply=%region_8.11 | all-reduce | flops 1024 | bytes 8192 | tf_op jit(solution)/shard_map/psum | solution.py:108
  487.8 0.8 convolution_subtract_fusion
  488.7 75.3 %psum.39 = f32[32,32]{0,1:T(8,128)S(1)} all-reduce(f32[32,32]{0,1:T(8,128)S(1)} %fusion.54), channel_id=1, replica_groups=mesh['loop'=4,'inner'=64] {'loop','inner'}, use_global_device_ids=true, to_apply=%region_9.12 | all-reduce | flops 1024 | bytes 8192 | tf_op jit(solution)/shard_map/psum | solution.py:112
  564.1 2.9 cholesky.81
  567.1 0.6 compare_reduce_fusion
  567.7 0.7 fusion.37
  568.4 2.4 custom-call.9
  571.1 0.6 pad_maximum_fusion.3
  571.7 0.7 copy.35
  (46 shorter events, 2.5 us)
Async XLA Ops:
  7.2 2.6 copy-start
  7.2 94.4 %all-gather.5.cloned.1.call-start = ((), (), s32[]{:S(2)}) async-start(), calls=%async_computation | async-start | bytes 2621440 | tf_op jit(solution)/shard_map/all_gather | solution.py:53
  101.5 48.3 %collective-permute-start.1 = (bf16[4,256,1024]{2,1,0:T(8,128)(2,1)}, bf16[4,256,1024]{2,1,0:T(8,128)(2,1)S(1)}, u32[]{:S(2)}, u32[]{:S(2)}) collective-permute-start(bf16[4,256,1024]{2,1,0:T(8,128)(2,1)} %bitcast.93), channel_id=1, source_target_pairs={{1,0},{2,1},{3,2},{4,3},{5,4},{6,5},{7,6},{8,7},{9,8},{10,9},{11,1... | collective-permute-start | bytes 6291464 | tf_op jit(solution)/shard_map/ppermute | solution.py:20
  102.8 91.7 %collective-permute-start = (bf16[4,256,1024]{2,1,0:T(8,128)(2,1)}, bf16[4,256,1024]{2,1,0:T(8,128)(2,1)}, u32[]{:S(2)}, u32[]{:S(2)}) collective-permute-start(bf16[4,256,1024]{2,1,0:T(8,128)(2,1)} %bitcast.94), channel_id=1, source_target_pairs={{0,1},{1,2},{2,3},{3,4},{4,5},{5,6},{6,7},{7,8},{8,9},{9,10},{10,1... | collective-permute-start | bytes 6291464 | tf_op jit(solution)/shard_map/ppermute | solution.py:18
  118.8 79.3 %copy-start.1 = (bf16[256,1024]{1,0:T(8,128)(2,1)S(1)}, bf16[256,1024]{1,0:T(8,128)(2,1)}, u32[]{:S(2)}) copy-start(bf16[256,1024]{1,0:T(8,128)(2,1)} %param.7) | copy-start | bytes 1572868
  204.8 185.5 %copy-start.5 = (f32[256]{0:T(256)}, f32[256]{0:T(256)S(1)}, u32[]{:S(2)}) copy-start(f32[256]{0:T(256)S(1)} %rsqrt.7) | copy-start | bytes 3076
  212.3 7.9 %collective-permute-start.3 = (f32[4,256,32]{1,0,2:T(4,128)S(1)}, f32[4,256,32]{1,0,2:T(4,128)S(1)}, u32[]{:S(2)}, u32[]{:S(2)}) collective-permute-start(f32[4,256,32]{1,0,2:T(4,128)S(1)} %reshape.60), channel_id=1, source_target_pairs={{1,0},{2,1},{3,2},{4,3},{5,4},{6,5},{7,6},{8,7},{9,8},{10,9},{11,1... | collective-permute-start | bytes 393224 | tf_op jit(solution)/shard_map/ppermute | solution.py:20
  213.6 9.8 %collective-permute-start.2 = (f32[4,256,32]{1,0,2:T(4,128)S(1)}, f32[4,256,32]{1,0,2:T(4,128)S(1)}, u32[]{:S(2)}, u32[]{:S(2)}) collective-permute-start(f32[4,256,32]{1,0,2:T(4,128)S(1)} %reshape.60), channel_id=1, source_target_pairs={{0,1},{1,2},{2,3},{3,4},{4,5},{5,6},{6,7},{7,8},{8,9},{9,10},{10,1... | collective-permute-start | bytes 393224 | tf_op jit(solution)/shard_map/ppermute | solution.py:18
  306.9 83.4 %copy-start.2 = (f32[32,32]{0,1:T(8,128)}, f32[32,32]{0,1:T(8,128)S(1)}, u32[]{:S(2)}) copy-start(f32[32,32]{0,1:T(8,128)S(1)} %psum.36) | copy-start | bytes 12292
  397.8 173.9 %copy-start.3 = (f32[32,32]{0,1:T(8,128)S(1)}, f32[32,32]{0,1:T(8,128)}, u32[]{:S(2)}) copy-start(f32[32,32]{0,1:T(8,128)} %copy-done.2) | copy-start | bytes 12292
  397.8 173.9 %copy-start.4 = (f32[1,32,32]{1,2,0:T(8,128)S(1)}, f32[1,32,32]{1,2,0:T(8,128)}, u32[]{:S(2)}) copy-start(f32[1,32,32]{1,2,0:T(8,128)} %get-tuple-element.12) | copy-start | bytes 12292
  397.8 6.8 %collective-permute-start.5 = (f32[4,256,32]{1,0,2:T(4,128)S(1)}, f32[4,256,32]{1,0,2:T(4,128)S(1)}, u32[]{:S(2)}, u32[]{:S(2)}) collective-permute-start(f32[4,256,32]{1,0,2:T(4,128)S(1)} %reshape.61), channel_id=1, source_target_pairs={{1,0},{2,1},{3,2},{4,3},{5,4},{6,5},{7,6},{8,7},{9,8},{10,9},{11,1... | collective-permute-start | bytes 393224 | tf_op jit(solution)/shard_map/ppermute | solution.py:20
  399.1 8.2 %collective-permute-start.4 = (f32[4,256,32]{1,0,2:T(4,128)S(1)}, f32[4,256,32]{1,0,2:T(4,128)S(1)}, u32[]{:S(2)}, u32[]{:S(2)}) collective-permute-start(f32[4,256,32]{1,0,2:T(4,128)S(1)} %reshape.61), channel_id=1, source_target_pairs={{0,1},{1,2},{2,3},{3,4},{4,5},{5,6},{6,7},{7,8},{8,9},{9,10},{10,1... | collective-permute-start | bytes 393224 | tf_op jit(solution)/shard_map/ppermute | solution.py:18
Sparse Core Ops, SparseCore 0:
  9.8 33.8 all-gather.4
where the time goes:
time: 581 us; the launch traced here: 579 us
  blocking collectives  413 us (71%)
  waiting for transfers between devices  85.5 us (15%)
  other arithmetic  26.3 us (5%)
  matrix products  18.7 us (3%)
  starting transfers between devices  17.9 us (3%)
  between operations  14.3 us (2%)
    psum x2, blocking collectives, local(): projected = lax.psum(local_gram(current, image), ('loop', 'inner'))  157 us
    psum x2, blocking collectives, local(): gram_total = lax.psum(local_gram(image, image), ('loop', 'inner'))  151 us
    psum x1, blocking collectives, local(): lax.psum(local_gram(start_block, start_block), ('loop', 'inner'))  90.2 us
    ppermute x3, waiting for transfers between devices, extended(): lax.ppermute(tail, axis, [(i, (i + 1) % count) for i in range(ends)])  50.5 us
    ppermute x3, waiting for transfers between devices, extended(): lax.ppermute(head, axis, [((i + 1) % count, i) for i in range(ends)])  34.4 us
    all_gather x2, blocking collectives, local(): vec_stack = lax.all_gather(scaled[None], 'loop', axis=0, tiled=True)  14.7 us
    ppermute x3, starting transfers between devices, extended(): lax.ppermute(tail, axis, [(i, (i + 1) % count) for i in range(ends)])  14 us
  transfers between devices with their start and end apart: 7, of which 6 were waited for; matrix products, arithmetic and copies ran while one was open for 2% of the time, Pallas kernels for 0%

commit v1 on v0

--- a/solution.py
+++ b/solution.py
@@ -2,6 +2,7 @@
 import jax.numpy as jnp
 from jax import lax
 from jax.sharding import PartitionSpec as P
+from jax.lax import psum
 
 STEPS = 2
 BINS_COL = 8
@@ -105,7 +106,7 @@
         strip = vec_strip.reshape(n_loop * 3 * row_count, block_width)
         total = jnp.dot(current_kernel(0), strip, precision=lax.Precision.HIGHEST)
         image = inv_root[:, None] * total
-        projected = lax.psum(local_gram(current, image), ("loop", "inner"))
+        projected = psum(psum(local_gram(current, image), "loop"), axis_name="inner")
         image = image - jnp.dot(current, projected, precision=lax.Precision.HIGHEST)
         if lanczos_step > 0:
             image = image - jnp.dot(previous, prev_b.T, precision=lax.Precision.HIGHEST)

time: 581 us -> 1060 us (1.82)
  blocking collectives: 413 us -> 896 us
    psum x2 -> x4, blocking collectives: 157 us -> 529 us  [the longest x2 504 us: local(): psum(psum(local_gram(current, image), 'loop'), axis_name='inner')]
    psum x2, blocking collectives: 151 us -> 262 us  [local(): gram_total = lax.psum(local_gram(image, image), ('loop', 'inner'))]
  transfers between devices with their start and end apart: 7 -> 7, of which waited for: 6 -> 6; matrix products, arithmetic and copies ran while one was open for 2% -> 1% of each run, Pallas kernels for 0% -> 0%
where the time goes in v1:
time: 1060 us
  blocking collectives  896 us (85%)
  waiting for transfers between devices  86.2 us (8%)
  other arithmetic  26.3 us (2%)
  matrix products  18.7 us (2%)
  starting transfers between devices  17.9 us (2%)
  between operations  14.3 us (1%)
    psum x2, blocking collectives, local(): psum(psum(local_gram(current, image), 'loop'), axis_name='inner')  504 us
    psum x2, blocking collectives, local(): gram_total = lax.psum(local_gram(image, image), ('loop', 'inner'))  262 us
    psum x1, blocking collectives, local(): lax.psum(local_gram(start_block, start_block), ('loop', 'inner'))  90.2 us
    ppermute x3, waiting for transfers between devices, extended(): lax.ppermute(tail, axis, [(i, (i + 1) % count) for i in range(ends)])  51.1 us
    ppermute x3, waiting for transfers between devices, extended(): lax.ppermute(head, axis, [((i + 1) % count, i) for i in range(ends)])  34.4 us
    psum x2, blocking collectives, local(): psum(local_gram(current, image), 'loop')  25.1 us
  transfers between devices with their start and end apart: 7, of which 6 were waited for; matrix products, arithmetic and copies ran while one was open for 1% of the time, Pallas kernels for 0%

profile of v1, /device:TPU:1, one launch (start us, length us, event | category | flops | bytes accessed | tf_op | source)
XLA Modules:
  0.0 1063.0 jit_solution(16362513395534886772)
XLA Ops:
  7.2 0.7 all-gather.5.cloned.1.call-update
  7.9 1.0 reshape.51
  9.0 0.8 dynamic_slice.6
  9.8 1.3 fusion.49
  11.2 90.2 %psum.49 = f32[32,32]{0,1:T(8,128)S(1)} all-reduce(f32[32,32]{0,1:T(8,128)S(1)} %fusion.50), channel_id=1, replica_groups=mesh['loop'=4,'inner'=64] {'loop','inner'}, use_global_device_ids=true, to_apply=%region_0.1 | all-reduce | flops 1024 | bytes 8192 | tf_op jit(solution)/shard_map/psum | solution.py:96
  101.5 1.3 collective-permute-start.1
  102.8 5.3 collective-permute-start
  108.1 2.9 cholesky.59
  111.1 0.6 compare_reduce_fusion.2
  111.7 0.7 fusion.30
  112.4 2.4 custom-call.7
  114.8 1.2 multiply_reduce_fusion.1
  116.1 0.8 fusion.45
  116.9 1.0 fusion.7
  117.9 1.0 fusion.4
  118.8 31.0 %collective-permute-done.1 = bf16[4,256,1024]{2,1,0:T(8,128)(2,1)S(1)} collective-permute-done((bf16[4,256,1024]{2,1,0:T(8,128)(2,1)}, bf16[4,256,1024]{2,1,0:T(8,128)(2,1)S(1)}, u32[]{:S(2)}, u32[]{:S(2)}) %collective-permute-start.1) | collective-permute-done | bytes 2097184 | tf_op jit(solution)/shard_map/ppermute | solution.py:21
  149.8 44.7 %collective-permute-done = bf16[4,256,1024]{2,1,0:T(8,128)(2,1)} collective-permute-done((bf16[4,256,1024]{2,1,0:T(8,128)(2,1)}, bf16[4,256,1024]{2,1,0:T(8,128)(2,1)}, u32[]{:S(2)}, u32[]{:S(2)}) %collective-permute-start) | collective-permute-done | bytes 2097184 | tf_op jit(solution)/shard_map/ppermute | solution.py:19
  194.5 3.6 multiply_reduce_fusion
  198.2 3.5 fusion
  201.7 3.1 fusion.46
  205.0 7.2 all-gather.1
  212.3 1.3 collective-permute-start.3
  213.6 4.8 collective-permute-start.2
  218.4 1.9 collective-permute-done.3
  220.2 3.2 collective-permute-done.2
  223.6 2.8 convolution_multiply_fusion.3
  226.5 12.5 %psum.50 = f32[32,32]{0,1:T(8,128)S(1)} all-reduce(f32[32,32]{0,1:T(8,128)S(1)} %fusion.51), channel_id=1, replica_groups=mesh['loop'=4,'inner'=64] {'loop'}, use_global_device_ids=true, to_apply=%region_6.9 | all-reduce | flops 1024 | bytes 8192 | tf_op jit(solution)/shard_map/psum | solution.py:109
  239.1 251.1 %psum.51 = f32[32,32]{0,1:T(8,128)S(1)} all-reduce(f32[32,32]{0,1:T(8,128)S(1)} %psum.50), channel_id=1, replica_groups=mesh['loop'=4,'inner'=64] {'inner'}, use_global_device_ids=true, to_apply=%region_7.10 | all-reduce | flops 1024 | bytes 8192 | tf_op jit(solution)/shard_map/psum | solution.py:109
  490.5 132.1 %psum.52 = f32[32,32]{0,1:T(8,128)S(1)} all-reduce(f32[32,32]{0,1:T(8,128)S(1)} %fusion.52), channel_id=1, replica_groups=mesh['loop'=4,'inner'=64] {'loop','inner'}, use_global_device_ids=true, to_apply=%region_8.11 | all-reduce | flops 1024 | bytes 8192 | tf_op jit(solution)/shard_map/psum | solution.py:113
  622.6 2.9 cholesky.70
  626.2 1.2 fusion.38
  627.3 2.4 custom-call.8
  630.1 7.4 all-gather.2
  637.6 1.3 collective-permute-start.5
  638.9 4.0 collective-permute-start.4
  642.9 1.5 collective-permute-done.5
  644.4 3.3 collective-permute-done.4
  647.8 3.5 convolution_multiply_fusion.2
  651.5 12.5 %psum.53 = f32[32,32]{0,1:T(8,128)S(1)} all-reduce(f32[32,32]{0,1:T(8,128)S(1)} %fusion.53), channel_id=1, replica_groups=mesh['loop'=4,'inner'=64] {'loop'}, use_global_device_ids=true, to_apply=%region_9.12 | all-reduce | flops 1024 | bytes 8192 | tf_op jit(solution)/shard_map/psum | solution.py:109
  664.0 252.7 %psum.54 = f32[32,32]{0,1:T(8,128)S(1)} all-reduce(f32[32,32]{0,1:T(8,128)S(1)} %psum.53), channel_id=1, replica_groups=mesh['loop'=4,'inner'=64] {'inner'}, use_global_device_ids=true, to_apply=%region_10.13 | all-reduce | flops 1024 | bytes 8192 | tf_op jit(solution)/shard_map/psum | solution.py:109
  916.9 0.8 convolution_subtract_fusion
  917.9 129.9 %psum.55 = f32[32,32]{0,1:T(8,128)S(1)} all-reduce(f32[32,32]{0,1:T(8,128)S(1)} %fusion.54), channel_id=1, replica_groups=mesh['loop'=4,'inner'=64] {'loop','inner'}, use_global_device_ids=true, to_apply=%region_11.14 | all-reduce | flops 1024 | bytes 8192 | tf_op jit(solution)/shard_map/psum | solution.py:113
  1047.8 2.9 cholesky.81
  1050.8 0.6 compare_reduce_fusion
  1051.4 0.7 fusion.37
  1052.1 2.4 custom-call.9
  1054.8 0.6 pad_maximum_fusion.3
  1055.4 0.7 copy.35
  (48 shorter events, 3.4 us)
Async XLA Ops:
  7.2 2.6 copy-start
  7.2 94.4 %all-gather.5.cloned.1.call-start = ((), (), s32[]{:S(2)}) async-start(), calls=%async_computation | async-start | bytes 2621440 | tf_op jit(solution)/shard_map/all_gather | solution.py:54
  101.5 48.3 %collective-permute-start.1 = (bf16[4,256,1024]{2,1,0:T(8,128)(2,1)}, bf16[4,256,1024]{2,1,0:T(8,128)(2,1)S(1)}, u32[]{:S(2)}, u32[]{:S(2)}) collective-permute-start(bf16[4,256,1024]{2,1,0:T(8,128)(2,1)} %bitcast.93), channel_id=1, source_target_pairs={{1,0},{2,1},{3,2},{4,3},{5,4},{6,5},{7,6},{8,7},{9,8},{10,9},{11,1... | collective-permute-start | bytes 6291464 | tf_op jit(solution)/shard_map/ppermute | solution.py:21
  102.8 91.7 %collective-permute-start = (bf16[4,256,1024]{2,1,0:T(8,128)(2,1)}, bf16[4,256,1024]{2,1,0:T(8,128)(2,1)}, u32[]{:S(2)}, u32[]{:S(2)}) collective-permute-start(bf16[4,256,1024]{2,1,0:T(8,128)(2,1)} %bitcast.94), channel_id=1, source_target_pairs={{0,1},{1,2},{2,3},{3,4},{4,5},{5,6},{6,7},{7,8},{8,9},{9,10},{10,1... | collective-permute-start | bytes 6291464 | tf_op jit(solution)/shard_map/ppermute | solution.py:19
  118.8 79.3 %copy-start.1 = (bf16[256,1024]{1,0:T(8,128)(2,1)S(1)}, bf16[256,1024]{1,0:T(8,128)(2,1)}, u32[]{:S(2)}) copy-start(bf16[256,1024]{1,0:T(8,128)(2,1)} %param.7) | copy-start | bytes 1572868
  204.8 425.3 %copy-start.5 = (f32[256]{0:T(256)}, f32[256]{0:T(256)S(1)}, u32[]{:S(2)}) copy-start(f32[256]{0:T(256)S(1)} %rsqrt.7) | copy-start | bytes 3076
  212.3 7.9 collective-permute-start.3
  213.6 9.8 collective-permute-start.2
  490.1 139.9 %copy-start.2 = (f32[32,32]{0,1:T(8,128)}, f32[32,32]{0,1:T(8,128)S(1)}, u32[]{:S(2)}) copy-start(f32[32,32]{0,1:T(8,128)S(1)} %psum.51) | copy-start | bytes 12292
  637.6 417.8 %copy-start.3 = (f32[32,32]{0,1:T(8,128)S(1)}, f32[32,32]{0,1:T(8,128)}, u32[]{:S(2)}) copy-start(f32[32,32]{0,1:T(8,128)} %copy-done.2) | copy-start | bytes 12292
  637.6 417.8 %copy-start.4 = (f32[1,32,32]{1,2,0:T(8,128)S(1)}, f32[1,32,32]{1,2,0:T(8,128)}, u32[]{:S(2)}) copy-start(f32[1,32,32]{1,2,0:T(8,128)} %get-tuple-element.12) | copy-start | bytes 12292
  637.6 6.8 collective-permute-start.5
  638.9 8.8 collective-permute-start.4
Sparse Core Ops, SparseCore 0:
  9.8 33.8 all-gather.4
